TPU v7x, 32 devices: a whole 2x2x4 slice. The times are simulated.
32 devices in a mesh: rows: 8 (over z, x), pre: 4 (over y, core).
Axes of the slice: x: 2, y: 2, z: 4, core: 2. Of those that a mesh axis runs over, the one named last changes fastest.
Arguments:
- tokens: bfloat16 [32, 1024, 1024], P(('rows', 'pre')), may hold values from -6 to 6
- seg_ids: int32 [32, 1024], P(('rows', 'pre')), may hold values from 0 to 7, never falling along the last dimension, each value on 1 to 256 neighbouring positions
- valid: int32 [32, 1024], P(('rows', 'pre')), may hold values from 0 to 1, as said below
- out_grad: bfloat16 [32, 1024, 1024], P(('rows', 'pre')), may hold values from -6 to 6
- ln1_gain: bfloat16 [1024], replicated, may hold values from 0.25 to 1.75
- ln1_bias: bfloat16 [1024], replicated, may hold values from -1.25 to 1.25
- qkv_weight: bfloat16 [1024, 3072], P(('rows', 'pre')), may hold values from -0.1875 to 0.1875
- qkv_bias: bfloat16 [3072], replicated, may hold values from -1.75 to 1.75
- proj_weight: bfloat16 [1024, 1024], P(('rows', 'pre')), may hold values from -0.5 to 0.5
- proj_bias: bfloat16 [1024], replicated, may hold values from -1.25 to 1.25
- ln2_gain: bfloat16 [1024], replicated, may hold values from 0.25 to 1.75
- ln2_bias: bfloat16 [1024], replicated, may hold values from -1.25 to 1.25
- fc_weight: bfloat16 [1024, 4096], P(('rows', 'pre')), may hold values from -0.1875 to 0.1875
- fc_bias: bfloat16 [4096], replicated, may hold values from -3 to 3
- out_weight: bfloat16 [4096, 1024], P(('rows', 'pre')), may hold values from -0.09375 to 0.09375
- out_bias: bfloat16 [1024], replicated, may hold values from -1.75 to 1.75
- prefix_emb: bfloat16 [10, 1024], replicated, may hold values from -6 to 6
- rep_weight1: bfloat16 [1024, 800], replicated, may hold values from -0.1875 to 0.1875
- rep_bias1: bfloat16 [800], replicated, may hold values from -3 to 3
- rep_weight2: bfloat16 [800, 2048], P(None, 'pre'), may hold values from -0.4375 to 0.4375
- rep_bias2: bfloat16 [2048], P('pre'), may hold values from -3 to 3
Outputs:
- output: bfloat16 [32, 1024, 1024], P(('rows', 'pre'))
- in_grad: bfloat16 [32, 1024, 1024], P(('rows', 'pre'))
- emb_grad: float32 [10, 1024], replicated
- rep_weight1_grad: float32 [1024, 800], replicated
- rep_bias1_grad: float32 [800], replicated
- rep_weight2_grad: float32 [800, 2048], P(None, 'pre')
- rep_bias2_grad: float32 [2048], P('pre')
Inputs may be any that keep to these rules, and one draw needn't show every extreme that they name: `seg_ids`: ids never fall along a row; each id covers 1 to 256 positions. `valid`: in each row, 1 on a leading run of 512 positions or more and 0 on the rest; every row ends in at least one 0.
All inputs are finite; a program needn't handle non-finite values.
Results may differ from a plain program's by a relative error of at most 0.019.
Values may be sent and summed in bfloat16 or wider, within the bound.
No kernel may reach another device: no remote copies, remote signals or barrier semaphores. Data moves between devices by JAX's collectives and lax.ppermute only.
A program may use at most 320 MiB of HBM per device.

v0:
```python
import jax
import jax.numpy as jnp
from jax import lax
from jax.sharding import PartitionSpec as P

D = 1024
H = 16
HD = 64


NEG = -1e30
EPS = 1e-05


def widen(array):
    return array.astype(jnp.float32)


def norm_rows(values, gain, shift):
    center = values - jnp.mean(values, axis=-1, keepdims=True)
    spread = jnp.mean(center * center, axis=-1, keepdims=True)
    return center * lax.rsqrt(spread + EPS) * gain + shift


def norm_grad(values, gain, shift, grad):

    def apply_norm(inner):
        return norm_rows(inner, gain, shift)

    _, pull_back = jax.vjp(apply_norm, values)
    return pull_back(grad)[0]


def gelu_tanh(values):
    return jax.nn.gelu(values, approximate=True)


def back_dot(grad, weight):
    return lax.dot_general(
        grad, weight, (((1,), (1,)), ((), ())), preferred_element_type=jnp.float32
    )


def mask_rows(seg_block, offset, seg_row, valid_row):
    query_place = offset + jnp.arange(seg_block.shape[0])
    key_place = jnp.arange(seg_row.shape[0])
    return (
        (seg_block[:, None] == seg_row[None, :])
        & (key_place[None, :] <= query_place[:, None])
        & (valid_row[None, :] > 0)
    )


def block_scores(q_block, keys, pkeys, allowed, scale):
    scores = jnp.einsum("qgd,kgd->gqk", q_block, keys, preferred_element_type=jnp.float32) * scale
    scores = jnp.where(allowed[None], scores, NEG)
    prefix_scores = (
        jnp.einsum("qgd,pgd->gqp", q_block, pkeys, preferred_element_type=jnp.float32) * scale
    )
    return (scores, prefix_scores)


def attend_forward(queries, keys, values, pkeys, pvalues, seg_row, valid_row):
    length, heads, width = queries.shape
    head_group = min(4, heads)
    block_rows = min(512, length)
    scale = float(width) ** (-0.5)

    def one_block(block_index):
        offset = block_index * block_rows
        q_block = lax.dynamic_slice_in_dim(queries, offset, block_rows, 0)
        allowed = mask_rows(
            lax.dynamic_slice_in_dim(seg_row, offset, block_rows, 0), offset, seg_row, valid_row
        )
        mix_parts = []
        lse_parts = []
        for head_first in range(0, heads, head_group):
            head_part = slice(head_first, head_first + head_group)
            scores, prefix_scores = block_scores(
                q_block[:, head_part], keys[:, head_part], pkeys[:, head_part], allowed, scale
            )
            highest = jnp.maximum(jnp.max(scores, axis=-1), jnp.max(prefix_scores, axis=-1))[
                ..., None
            ]
            exp_scores = jnp.exp(scores - highest)
            exp_prefix = jnp.exp(prefix_scores - highest)
            row_total = jnp.sum(exp_scores, axis=-1, keepdims=True) + jnp.sum(
                exp_prefix, axis=-1, keepdims=True
            )
            attn_probs = (exp_scores / row_total).astype(jnp.bfloat16)
            prefix_probs = (exp_prefix / row_total).astype(jnp.bfloat16)
            attn_mix = jnp.einsum(
                "gqk,kgd->qgd", attn_probs, values[:, head_part], preferred_element_type=jnp.float32
            )
            attn_mix = attn_mix + jnp.einsum(
                "gqp,pgd->qgd",
                prefix_probs,
                pvalues[:, head_part],
                preferred_element_type=jnp.float32,
            )
            mix_parts.append(attn_mix)
            lse_parts.append((highest + jnp.log(row_total))[..., 0])
        return (jnp.concatenate(mix_parts, 1), jnp.concatenate(lse_parts, 0))

    attn_mix, logsum = lax.map(one_block, jnp.arange(length // block_rows))
    return (attn_mix.reshape(length, heads * width), logsum)


def attend_backward(queries, keys, values, pkeys, pvalues, seg_row, valid_row, logsum, grad_mix):
    length, heads, width = queries.shape
    head_group = min(4, heads)
    block_rows = min(512, length)
    scale = float(width) ** (-0.5)

    def one_block(carry, block_index):
        grad_keys, grad_values, grad_pkeys, grad_pvalues = carry
        offset = block_index * block_rows
        q_block = lax.dynamic_slice_in_dim(queries, offset, block_rows, 0)
        g_block = lax.dynamic_slice_in_dim(grad_mix, offset, block_rows, 0)
        allowed = mask_rows(
            lax.dynamic_slice_in_dim(seg_row, offset, block_rows, 0), offset, seg_row, valid_row
        )
        row_lse = logsum[block_index]
        query_parts = []
        for head_first in range(0, heads, head_group):
            head_part = slice(head_first, head_first + head_group)
            scores, prefix_scores = block_scores(
                q_block[:, head_part], keys[:, head_part], pkeys[:, head_part], allowed, scale
            )
            lse_part = row_lse[head_part][..., None]
            attn_probs = jnp.exp(scores - lse_part)
            prefix_probs = jnp.exp(prefix_scores - lse_part)
            grad_probs = jnp.einsum(
                "qgd,kgd->gqk",
                g_block[:, head_part],
                values[:, head_part],
                preferred_element_type=jnp.float32,
            )
            grad_pprobs = jnp.einsum(
                "qgd,pgd->gqp",
                g_block[:, head_part],
                pvalues[:, head_part],
                preferred_element_type=jnp.float32,
            )
            row_dot = jnp.sum(attn_probs * grad_probs, axis=-1, keepdims=True) + jnp.sum(
                prefix_probs * grad_pprobs, axis=-1, keepdims=True
            )
            grad_scores = (attn_probs * (grad_probs - row_dot)).astype(jnp.bfloat16)
            grad_pscores = (prefix_probs * (grad_pprobs - row_dot)).astype(jnp.bfloat16)
            grad_query = jnp.einsum(
                "gqk,kgd->qgd", grad_scores, keys[:, head_part], preferred_element_type=jnp.float32
            )
            grad_query = (
                grad_query
                + jnp.einsum(
                    "gqp,pgd->qgd",
                    grad_pscores,
                    pkeys[:, head_part],
                    preferred_element_type=jnp.float32,
                )
            ) * scale
            query_parts.append(grad_query)
            grad_keys = grad_keys.at[:, head_part].add(
                jnp.einsum(
                    "gqk,qgd->kgd",
                    grad_scores,
                    q_block[:, head_part],
                    preferred_element_type=jnp.float32,
                )
                * scale
            )
            grad_values = grad_values.at[:, head_part].add(
                jnp.einsum(
                    "gqk,qgd->kgd",
                    attn_probs.astype(jnp.bfloat16),
                    g_block[:, head_part],
                    preferred_element_type=jnp.float32,
                )
            )
            grad_pkeys = grad_pkeys.at[:, head_part].add(
                jnp.einsum(
                    "gqp,qgd->pgd",
                    grad_pscores,
                    q_block[:, head_part],
                    preferred_element_type=jnp.float32,
                )
                * scale
            )
            grad_pvalues = grad_pvalues.at[:, head_part].add(
                jnp.einsum(
                    "gqp,qgd->pgd",
                    prefix_probs.astype(jnp.bfloat16),
                    g_block[:, head_part],
                    preferred_element_type=jnp.float32,
                )
            )
        return ((grad_keys, grad_values, grad_pkeys, grad_pvalues), jnp.concatenate(query_parts, 1))

    token_zeros = jnp.zeros(queries.shape, jnp.float32)
    prefix_zeros = jnp.zeros(pkeys.shape, jnp.float32)
    sums, grad_queries = lax.scan(
        one_block,
        (token_zeros, token_zeros, prefix_zeros, prefix_zeros),
        jnp.arange(length // block_rows),
    )
    return (sums, grad_queries.reshape(length, heads * width))


def per_device(
    tokens,
    seg_ids,
    valid,
    out_grad,
    ln1_gain,
    ln1_bias,
    qkv_weight,
    qkv_bias,
    proj_weight,
    proj_bias,
    ln2_gain,
    ln2_bias,
    fc_weight,
    fc_bias,
    out_weight,
    out_bias,
    prefix_emb,
    rep_weight1,
    rep_bias1,
    rep_weight2,
    rep_bias2,
):
    model = D
    head_width = HD
    row_count, length = (tokens.shape[0], tokens.shape[1])
    gain_one, shift_one = (widen(ln1_gain), widen(ln1_bias))
    gain_two, shift_two = (widen(ln2_gain), widen(ln2_bias))
    pre_hidden = jnp.dot(prefix_emb, rep_weight1, preferred_element_type=jnp.float32) + widen(
        rep_bias1
    )
    hidden = jnp.tanh(pre_hidden)
    hidden_low = hidden.astype(jnp.bfloat16)
    kv_local = (
        jnp.dot(hidden_low, rep_weight2, preferred_element_type=jnp.float32) + widen(rep_bias2)
    ).astype(jnp.bfloat16)
    prefix_kv = lax.all_gather(kv_local, "pre", axis=1, tiled=True)
    prefix_len = prefix_kv.shape[0]
    pkeys = prefix_kv[:, :model].reshape(prefix_len, H, head_width)
    pvalues = prefix_kv[:, model:].reshape(prefix_len, H, head_width)
    w_qkv, w_proj = (
        lax.all_gather(qkv_weight, ("rows", "pre"), axis=0, tiled=True),
        lax.all_gather(proj_weight, ("rows", "pre"), axis=0, tiled=True),
    )
    w_fc, w_out = (
        lax.all_gather(fc_weight, ("rows", "pre"), axis=0, tiled=True),
        lax.all_gather(out_weight, ("rows", "pre"), axis=0, tiled=True),
    )
    row_index = 0
    inputs = widen(tokens[row_index])
    normed1 = norm_rows(inputs, gain_one, shift_one).astype(jnp.bfloat16)
    qkv = (jnp.dot(normed1, w_qkv, preferred_element_type=jnp.float32) + widen(qkv_bias)).astype(
        jnp.bfloat16
    )
    queries = qkv[:, :model].reshape(length, H, head_width)
    keys = qkv[:, model : 2 * model].reshape(length, H, head_width)
    values = qkv[:, 2 * model :].reshape(length, H, head_width)
    attn_mix, logsum = attend_forward(
        queries, keys, values, pkeys, pvalues, seg_ids[row_index], valid[row_index]
    )
    attn_low = attn_mix.astype(jnp.bfloat16)
    middle = inputs + (
        jnp.dot(attn_low, w_proj, preferred_element_type=jnp.float32) + widen(proj_bias)
    )
    normed2 = norm_rows(middle, gain_two, shift_two).astype(jnp.bfloat16)
    pre_act = jnp.dot(normed2, w_fc, preferred_element_type=jnp.float32) + widen(fc_bias)
    act_low = gelu_tanh(pre_act).astype(jnp.bfloat16)
    result = middle + (
        jnp.dot(act_low, w_out, preferred_element_type=jnp.float32) + widen(out_bias)
    )
    outputs = [result.astype(jnp.bfloat16)]
    saved = [(inputs, queries, keys, values, logsum, middle, pre_act)]
    back_fc, back_out = (
        lax.all_gather(fc_weight, ("rows", "pre"), axis=0, tiled=True),
        lax.all_gather(out_weight, ("rows", "pre"), axis=0, tiled=True),
    )
    back_qkv, back_proj = (
        lax.all_gather(qkv_weight, ("rows", "pre"), axis=0, tiled=True),
        lax.all_gather(proj_weight, ("rows", "pre"), axis=0, tiled=True),
    )
    row_index = 0
    inputs, queries, keys, values, logsum, middle, pre_act = saved[row_index]
    grad_act = back_dot(out_grad[row_index], back_out)
    _, gelu_back = jax.vjp(gelu_tanh, pre_act)
    grad_pre = gelu_back(grad_act)[0].astype(jnp.bfloat16)
    grad_norm2 = back_dot(grad_pre, back_fc)
    grad_mid = widen(out_grad[row_index]) + norm_grad(middle, gain_two, shift_two, grad_norm2)
    grad_attn = back_dot(grad_mid.astype(jnp.bfloat16), back_proj).astype(jnp.bfloat16)
    sums, grad_queries = attend_backward(
        queries,
        keys,
        values,
        pkeys,
        pvalues,
        seg_ids[row_index],
        valid[row_index],
        logsum,
        grad_attn.reshape(length, H, head_width),
    )
    grad_keys, grad_values, grad_pkeys, grad_pvalues = sums
    grad_qkv = jnp.concatenate(
        [grad_queries, grad_keys.reshape(length, model), grad_values.reshape(length, model)], 1
    ).astype(jnp.bfloat16)
    grad_norm1 = back_dot(grad_qkv, back_qkv)
    grad_in = grad_mid + norm_grad(inputs, gain_one, shift_one, grad_norm1)
    in_grads = [grad_in.astype(jnp.bfloat16)]
    prefix_grad = jnp.concatenate(
        [grad_pkeys.reshape(prefix_len, model), grad_pvalues.reshape(prefix_len, model)], 1
    )
    summed = lax.psum(prefix_grad.astype(jnp.bfloat16), "rows")
    kv_grad = lax.psum_scatter(summed, "pre", scatter_dimension=1, tiled=True).astype(jnp.float32)
    kv_low = kv_grad.astype(jnp.bfloat16)
    bias2_grad = jnp.sum(widen(kv_low), axis=0)
    weight2_grad = lax.dot_general(
        hidden_low, kv_low, (((0,), (0,)), ((), ())), preferred_element_type=jnp.float32
    )
    hidden_part = back_dot(kv_low, rep_weight2)
    hid_grad = lax.psum(hidden_part, "pre")
    pre_grad = (hid_grad * (1.0 - hidden * hidden)).astype(jnp.bfloat16)
    bias1_grad = jnp.sum(widen(pre_grad), axis=0)
    weight1_grad = lax.dot_general(
        prefix_emb, pre_grad, (((0,), (0,)), ((), ())), preferred_element_type=jnp.float32
    )
    emb_grad = back_dot(pre_grad, rep_weight1)
    return (
        jnp.stack(outputs),
        jnp.stack(in_grads),
        emb_grad,
        weight1_grad,
        bias1_grad,
        weight2_grad,
        bias2_grad,
    )


def solution(mesh):
    return jax.shard_map(
        per_device,
        mesh=mesh,
        in_specs=(
            P(("rows", "pre"), None, None),
            P(("rows", "pre"), None),
            P(("rows", "pre"), None),
            P(("rows", "pre"), None, None),
            P(),
            P(),
            P(("rows", "pre"), None),
            P(),
            P(("rows", "pre"), None),
            P(),
            P(),
            P(),
            P(("rows", "pre"), None),
            P(),
            P(("rows", "pre"), None),
            P(),
            P(),
            P(),
            P(),
            P(None, "pre"),
            P("pre"),
        ),
        out_specs=(
            P(("rows", "pre"), None, None),
            P(("rows", "pre"), None, None),
            P(),
            P(),
            P(),
            P(None, "pre"),
            P("pre"),
        ),
        check_vma=False,
    )
```

profile of v0, /device:TPU:0, one launch (start us, length us, event | category | flops | bytes accessed | tf_op | source)
XLA Modules:
  0.0 725.8 jit_solution(12574365166061595942)
XLA Ops:
  23.2 6.2 all_gather.20
  29.6 3.9 copy.43
  41.7 41.4 %all-gather.5.cloned.1.call-done = bf16[1024,3072]{1,0:T(8,128)(2,1)} async-done(((bf16[32,3072]{1,0:T(8,128)(2,1)}), bf16[1024,3072]{1,0:T(8,128)(2,1)}) %all-gather.5.cloned.1.call-update) | async-done | bytes 6291472 | tf_op jit(solution)/shard_map/all_gather | solution.py:250
  83.1 10.6 %add_convert_fusion = bf16[1024,3072]{1,0:T(8,128)(2,1)S(1)} fusion(f32[3072]{0:T(1024)S(1)} %convert_element_type.232, bf16[1024,3072]{1,0:T(8,128)(2,1)} %all-gather.5.cloned.1.call-done, bf16[1,1024,1024]{1,2,0:T(8,128)(2,1)} %copy.43, f32[1024]{0:T(1024)S(1)} %convert_element_type.230, f32[1024]{0:T(1024)S(1)} %convert_element_type.229, ...), kind=kOutput, calls=%fused_computation.300 | convolution fusion | flops 6455033856 | bytes 14708736 | tf_op jit(solution)/shard_map/dot_general | solution.py:260
  100.5 4.0 copy.45
  104.5 4.0 copy.44
  110.0 129.8 %while.49 = (s32[]{:T(128)}, bf16[2,512,16,64]{1,3,2,0:T(8,128)(2,1)}, f32[2,16,512]{2,1,0:T(8,128)S(1)}, s32[2]{0:T(128)S(1)}, s32[1024]{0:T(1024)S(1)}, /*inde...) while((s32[]{:T(128)}, ...), condition=%wide.region_19.20_spmd, body=%wide.region_2.19_spmd.sunk | while | flops 2277049856 | bytes 235819504 | solution.py:105
  129.4 4.5 fusion.482
  133.9 4.5 fusion.478
  138.5 5.2 fusion.480
  143.7 11.7 %fusion.483 = (f32[4,512]{1,0:T(4,128)S(1)}, f32[4,512]{1,0:T(4,128)S(1)}, f32[4,512]{1,0:T(4,128)S(1)}, f32[4,512]{1,0:T(4,128)S(1)}, f32[4,512,1024]{2,1,0:T(8,128)S(1)}) fusion(f32[4,512,1024]{2,1,0:T(8,128)} %get-tuple-element.937, f32[4,512]{1,0:T(4,128)S(1)} %max.40, pred[512,1024]{1,0:T(8,128)(4,1)S(1)} %fusion.479, ...), kind=kOutput, calls=%fused_computation.16.clone.1 | convolution fusion | flops 295690240 | bytes 35692548 | tf_op jit(solution)/shard_map/while/body/eval_jaxpr/qgd,kgd->gqk/dot_general | solution.py:55
  155.6 9.7 %fusion.487 = (f32[4,512]{1,0:T(4,128)S(1)}, f32[4,512]{1,0:T(4,128)S(1)}, f32[4,512]{1,0:T(4,128)S(1)}) fusion(f32[4,512,1024]{2,1,0:T(8,128)S(1)} %get-tuple-element.942, f32[4,512]{1,0:T(4,128)S(1)} %max.42, pred[512,1024]{1,0:T(8,128)(4,1)S(1)} %fusion.479, f32[4,512]{1,0:T(4,128)S(1)} %max.43, f32[4,512,1024]{2,1,0:T(8,128)} %fusion.482, ...), kind=kLoop, calls=%fused_computation.17.clone.1 | loop fusion | flops 25159680 | bytes 25739264 | tf_op jit(solution)/shard_map/while/body/eval_jaxpr/reduce_sum | solution.py:87
  165.4 5.0 fusion.492
  186.6 5.2 fusion.482
  191.8 4.5 fusion.478
  196.4 5.2 fusion.480
  201.6 11.7 %fusion.483 = (f32[4,512]{1,0:T(4,128)S(1)}, f32[4,512]{1,0:T(4,128)S(1)}, f32[4,512]{1,0:T(4,128)S(1)}, f32[4,512]{1,0:T(4,128)S(1)}, f32[4,512,1024]{2,1,0:T(8,128)S(1)}) fusion(f32[4,512,1024]{2,1,0:T(8,128)} %get-tuple-element.937, f32[4,512]{1,0:T(4,128)S(1)} %max.40, pred[512,1024]{1,0:T(8,128)(4,1)S(1)} %fusion.479, ...), kind=kOutput, calls=%fused_computation.16.clone.1 | convolution fusion | flops 295690240 | bytes 35692548 | tf_op jit(solution)/shard_map/while/body/eval_jaxpr/qgd,kgd->gqk/dot_general | solution.py:55
  213.6 10.2 %fusion.487 = (f32[4,512]{1,0:T(4,128)S(1)}, f32[4,512]{1,0:T(4,128)S(1)}, f32[4,512]{1,0:T(4,128)S(1)}) fusion(f32[4,512,1024]{2,1,0:T(8,128)S(1)} %get-tuple-element.942, f32[4,512]{1,0:T(4,128)S(1)} %max.42, pred[512,1024]{1,0:T(8,128)(4,1)S(1)} %fusion.479, f32[4,512]{1,0:T(4,128)S(1)} %max.43, f32[4,512,1024]{2,1,0:T(8,128)} %fusion.482, ...), kind=kLoop, calls=%fused_computation.17.clone.1 | loop fusion | flops 25159680 | bytes 25739264 | tf_op jit(solution)/shard_map/while/body/eval_jaxpr/reduce_sum | solution.py:87
  223.9 5.0 fusion.492
  245.5 5.7 fusion.310
  253.7 17.5 %fusion.261 = f32[1024,4096]{1,0:T(8,128)} fusion(bf16[1024,4096]{1,0:T(8,128)(2,1)} %all-gather.9.cloned.1.call-done, f32[1024,1024]{0,1:T(8,128)} %copy-done.13, f32[1024]{0:T(1024)S(1)} %copy-done.49, f32[1024]{0:T(1024)S(1)} %copy-done.43, f32[1024]{0:T(1024)S(1)} %fusion.291, f32[1024]{0:T(1024)S(1)} %broadcast_multiply_fusion), kind=kOutput, calls=%fused_computation.332 | convolution fusion | flops 8595177472 | bytes 29376512 | tf_op jit(solution)/shard_map/dot_general | solution.py:274
  271.2 28.0 %all-gather.11.cloned.1.call-done = bf16[4096,1024]{1,0:T(8,128)(2,1)} async-done(((bf16[128,1024]{1,0:T(8,128)(2,1)}), bf16[4096,1024]{1,0:T(8,128)(2,1)}) %all-gather.11.cloned.1.call-update) | async-done | bytes 8388624 | tf_op jit(solution)/shard_map/all_gather | solution.py:255
  299.2 30.3 %multiply_reduce_fusion.8 = (f32[1024]{0:T(1024)S(1)}, f32[1024,1024]{0,1:T(8,128)}) fusion(f32[1024,1024]{0,1:T(8,128)} %copy-done.13, f32[1024]{0:T(1024)S(1)} %copy-done.43, f32[1024]{0:T(1024)S(1)} %broadcast_multiply_fusion, bf16[1024,4096]{1,0:T(8,128)(2,1)} %all-gather.9.cloned.1.call-done, f32[1024,4096]{1,0:T(8,128)} %fusion.261, ...), kind=kOutput, calls=%fused_computation.326 | convolution fusion | flops 17272143872 | bytes 44068864 | tf_op jit(solution)/shard_map/dot_general | solution.py:39
  329.5 4.7 fusion.303
  344.6 266.0 %while.50 = (s32[]{:T(128)}, f32[1024,16,64]{0,2,1:T(8,128)}, f32[1024,16,64]{0,2,1:T(8,128)}, f32[10,16,64]{2,0,1:T(8,128)S(1)}, f32[10,16,64]{2,0,1:T(8,128)S(...) while((s32[]{:T(128)}, f32[1024,16,64]{0,2,1:T(8,128)}, ...), condition=%wide.region_33.34_spmd, body=%wide.region_24.33_spmd.sunk | while | flops 5558656512 | bytes 617108288 | solution.py:201
  380.8 4.5 fusion.550
  385.3 4.5 fusion.548
  389.8 5.0 fusion.562
  402.0 4.6 fusion.551
  406.6 4.5 fusion.549
  411.1 4.5 fusion.547
  415.6 23.9 %multiply_reduce_fusion.15 = (f32[4,512]{1,0:T(4,128)S(1)}, f32[4,512]{1,0:T(4,128)S(1)}, f32[4,512]{1,0:T(4,128)S(1)}, f32[4,512]{1,0:T(4,128)S(1)}, f32[4,512,1024]{2,1,0:T(8,128)}) fusion(f32[4,512,1024]{2,1,0:T(8,128)} %copy-done.5, f32[4,512]{1,0:T(4,128)S(1)} %get-tuple-element.980, pred[512,1024]{1,0:T(8,128)(4,1)S(1)} %fusion.546, ...), kind=kOutput, calls=%fused_computation.114.clone.1 | convolution fusion | flops 310370304 | bytes 69271552 | tf_op jit(solution)/shard_map/while/body/eval_jaxpr/qgd,kgd->gqk/dot_general | solution.py:133
  439.7 27.8 %multiply_convert_fusion.19 = (bf16[4,512,1024]{2,1,0:T(8,128)(2,1)S(1)}, bf16[4,512,1024]{2,1,0:T(8,128)(2,1)}, bf16[4,512,1024]{2,1,0:T(8,128)(2,1)}, bf16[4,512,1024]{2,1,0:T(8,128)(2,1)}) fusion(f32[4,512,1024]{2,1,0:T(8,128)} %get-tuple-element.984, f32[4,512,1024]{2,1,0:T(8,128)} %copy-done.5, f32[4,512]{1,0:T(4,128)S(1)} %add.821, ...), kind=kLoop, calls=%fused_computation.113.clone.1 | loop fusion | flops 50331648 | bytes 84475904 | tf_op jit(solution)/shard_map/while/body/eval_jaxpr/convert_element_type | solution.py:148
  500.0 4.5 fusion.550
  504.6 4.5 fusion.548
  509.1 5.0 fusion.562
  521.3 4.6 fusion.551
  525.9 4.5 fusion.549
  530.4 4.5 fusion.547
  534.9 23.9 %multiply_reduce_fusion.15 = (f32[4,512]{1,0:T(4,128)S(1)}, f32[4,512]{1,0:T(4,128)S(1)}, f32[4,512]{1,0:T(4,128)S(1)}, f32[4,512]{1,0:T(4,128)S(1)}, f32[4,512,1024]{2,1,0:T(8,128)}) fusion(f32[4,512,1024]{2,1,0:T(8,128)} %copy-done.5, f32[4,512]{1,0:T(4,128)S(1)} %get-tuple-element.980, pred[512,1024]{1,0:T(8,128)(4,1)S(1)} %fusion.546, ...), kind=kOutput, calls=%fused_computation.114.clone.1 | convolution fusion | flops 310370304 | bytes 69271552 | tf_op jit(solution)/shard_map/while/body/eval_jaxpr/qgd,kgd->gqk/dot_general | solution.py:133
  559.0 27.8 %multiply_convert_fusion.19 = (bf16[4,512,1024]{2,1,0:T(8,128)(2,1)S(1)}, bf16[4,512,1024]{2,1,0:T(8,128)(2,1)}, bf16[4,512,1024]{2,1,0:T(8,128)(2,1)}, bf16[4,512,1024]{2,1,0:T(8,128)(2,1)}) fusion(f32[4,512,1024]{2,1,0:T(8,128)} %get-tuple-element.984, f32[4,512,1024]{2,1,0:T(8,128)} %copy-done.5, f32[4,512]{1,0:T(4,128)S(1)} %add.821, ...), kind=kLoop, calls=%fused_computation.113.clone.1 | loop fusion | flops 50331648 | bytes 84475904 | tf_op jit(solution)/shard_map/while/body/eval_jaxpr/convert_element_type | solution.py:148
  622.4 9.5 %fusion.257 = (f32[1024]{0:T(1024)S(1)}, f32[1024,1024]{0,1:T(8,128)S(1)}) fusion(bf16[1,1024,1024]{1,2,0:T(8,128)(2,1)S(1)} %copy-done.12, f32[1024]{0:T(1024)S(1)} %copy-done.40, f32[1024]{0:T(1024)S(1)} %copy-done.36, bf16[1024,3072]{1,0:T(8,128)(2,1)} %all-gather.5.cloned.1.call-done, bf16[1024,1024]{0,1:T(8,128)(2,1)S(1)} %bitcast.349, ...), kind=kOutput, calls=%fused_computation.323 | convolution fusion | flops 6466567168 | bytes 18886656 | tf_op jit(solution)/shard_map/dot_general | solution.py:39
  633.9 17.4 %fusion.262 = bf16[1,1024,1024]{1,2,0:T(8,128)(2,1)} fusion(f32[1024,1024]{0,1:T(8,128)} %copy-done.13, f32[1024]{0:T(1024)S(1)} %copy-done.48, bf16[4096,1024]{1,0:T(8,128)(2,1)} %all-gather.11.cloned.1.call-done, f32[1024,4096]{1,0:T(8,128)} %fusion.261, f32[4096]{0:T(1024)S(1)} %copy-done.45), kind=kOutput, calls=%fused_computation.333 | convolution fusion | flops 8635023360 | bytes 31477760 | tf_op jit(solution)/shard_map/dot_general | solution.py:277
  651.3 6.7 fusion.263
  658.1 4.0 copy.57
  662.1 3.9 copy.58
  666.0 35.6 %psum.16 = bf16[10,512]{1,0:T(8,128)(2,1)S(1)} all-reduce(bf16[10,512]{1,0:T(8,128)(2,1)} %reduce-scatter.2.cloned.1.call-done), channel_id=1, replica_groups=mesh['rows'=8,'pre'=4] {'rows'}, use_global_device_ids=true, to_apply=%region_36.37 | all-reduce | flops 5120 | bytes 20480 | tf_op jit(solution)/shard_map/psum | solution.py:318
  704.1 11.0 %psum.15 = f32[10,800]{1,0:T(8,128)S(1)} all-reduce(f32[10,800]{1,0:T(8,128)S(1)} %fusion.313), channel_id=1, replica_groups=mesh['rows'=8,'pre'=4] {'pre'}, use_global_device_ids=true, to_apply=%region_38.39 | all-reduce | flops 8000 | bytes 64000 | tf_op jit(solution)/shard_map/psum | solution.py:326
  (402 shorter events, 176.7 us)
Async XLA Ops:
  7.2 12.7 %copy-start = (bf16[1024,800]{0,1:T(8,128)(2,1)S(1)}, bf16[1024,800]{0,1:T(8,128)(2,1)}, u32[]{:S(2)}) copy-start(bf16[1024,800]{0,1:T(8,128)(2,1)} %param.74) | copy-start | bytes 4915204
  7.2 75.9 %all-gather.5.cloned.1.call-start = ((), (), s32[]{:S(2)}) async-start(), calls=%async_computation.1 | async-start | bytes 6488064 | tf_op jit(solution)/shard_map/all_gather | solution.py:250
  7.9 237.6 %all-gather.7.cloned.1.call-start = ((), (), s32[]{:S(2)}) async-start(), calls=%async_computation.2 | async-start | bytes 2162688 | tf_op jit(solution)/shard_map/all_gather | solution.py:251
  8.7 245.0 %all-gather.9.cloned.1.call-start = ((), (), s32[]{:S(2)}) async-start(), calls=%async_computation.3 | async-start | bytes 8650752 | tf_op jit(solution)/shard_map/all_gather | solution.py:254
  9.4 289.8 %all-gather.11.cloned.1.call-start = ((), (), s32[]{:S(2)}) async-start(), calls=%async_computation.4 | async-start | bytes 8650752 | tf_op jit(solution)/shard_map/all_gather | solution.py:255
  10.0 656.1 %reduce-scatter.2.cloned.1.call-start = ((), (), s32[]{:S(2)}) async-start(), calls=%async_computation.5 | async-start | bytes 81920 | tf_op jit(solution)/shard_map/reduce_scatter | solution.py:319
  11.4 71.7 %copy-start.39 = (f32[1024]{0:T(1024)}, f32[1024]{0:T(1024)S(1)}, u32[]{:S(2)}) copy-start(f32[1024]{0:T(1024)S(1)} %convert_element_type.229) | copy-start | bytes 12292
  35.6 58.2 %copy-start.35 = (f32[1024]{0:T(1024)}, f32[1024]{0:T(1024)S(1)}, u32[]{:S(2)}) copy-start(f32[1024]{0:T(1024)S(1)} %broadcast_multiply_fusion.1) | copy-start | bytes 12292
  37.8 56.0 %copy-start.37 = (f32[1024]{0:T(1024)}, f32[1024]{0:T(1024)S(1)}, u32[]{:S(2)}) copy-start(f32[1024]{0:T(1024)S(1)} %fusion.253) | copy-start | bytes 12292
  37.8 56.0 %copy-start.41 = (f32[1024]{0:T(1024)}, f32[1024]{0:T(1024)S(1)}, u32[]{:S(2)}) copy-start(f32[1024]{0:T(1024)S(1)} %fusion.290) | copy-start | bytes 12292
  104.5 5.5 copy-start.30
  104.5 5.5 copy-start.33
  124.7 3.9 copy-start.1
  124.7 4.7 copy-start.9
  155.6 9.8 %copy-start.21 = (bf16[1024,16,64]{0,2,1:T(8,128)(2,1)S(1)}, bf16[1024,16,64]{0,2,1:T(8,128)(2,1)}, u32[]{:S(2)}) copy-start(bf16[1024,16,64]{0,2,1:T(8,128)(2,1)} %get-tuple-element.1043) | copy-start | bytes 6291460 | tf_op jit(solution)/shard_map/while
  155.6 15.0 %slice-start.2 = ((s8[8388608]{0:T(1024)(128)(4,1)}), s8[4194304]{0:T(1024)(128)(4,1)S(1)}, s32[]{:S(2)}) async-start(s8[8388608]{0:T(1024)(128)(4,1)} %bitcast.342), calls=%async_computation.8 | async-start | bytes 8388608 | tf_op jit(solution)/shard_map/while
  165.4 5.3 slice-start.3
  165.4 8.2 %slice-start.4 = ((s8[8388608]{0:T(1024)(128)(4,1)}), s8[4194304]{0:T(1024)(128)(4,1)S(1)}, s32[]{:S(2)}) async-start(s8[8388608]{0:T(1024)(128)(4,1)} %bitcast.360), calls=%async_computation.10 | async-start | bytes 8388608 | tf_op jit(solution)/shard_map/while
  182.1 3.7 copy-start.1
  182.1 4.5 copy-start.9
  213.6 10.3 %copy-start.21 = (bf16[1024,16,64]{0,2,1:T(8,128)(2,1)S(1)}, bf16[1024,16,64]{0,2,1:T(8,128)(2,1)}, u32[]{:S(2)}) copy-start(bf16[1024,16,64]{0,2,1:T(8,128)(2,1)} %get-tuple-element.1043) | copy-start | bytes 6291460 | tf_op jit(solution)/shard_map/while
  213.6 15.5 %slice-start.2 = ((s8[8388608]{0:T(1024)(128)(4,1)}), s8[4194304]{0:T(1024)(128)(4,1)S(1)}, s32[]{:S(2)}) async-start(s8[8388608]{0:T(1024)(128)(4,1)} %bitcast.342), calls=%async_computation.8 | async-start | bytes 8388608 | tf_op jit(solution)/shard_map/while
  223.9 5.3 slice-start.3
  223.9 8.2 %slice-start.4 = ((s8[8388608]{0:T(1024)(128)(4,1)}), s8[4194304]{0:T(1024)(128)(4,1)S(1)}, s32[]{:S(2)}) async-start(s8[8388608]{0:T(1024)(128)(4,1)} %bitcast.360), calls=%async_computation.10 | async-start | bytes 8388608 | tf_op jit(solution)/shard_map/while
  239.8 5.7 copy-start.50
  253.6 45.5 %copy-start.44 = (f32[4096]{0:T(1024)S(1)}, f32[4096]{0:T(1024)}, u32[]{:S(2)}) copy-start(f32[4096]{0:T(1024)} %convert_element_type.244) | copy-start | bytes 49156
  329.5 4.7 copy-start.27
  329.5 4.7 copy-start.51
  334.2 3.8 copy-start.14
  334.3 3.8 copy-start.46
  368.4 4.7 copy-start.2
  368.4 5.1 copy-start.3
  385.3 9.5 %slice-start = ((s8[8388608]{0:T(1024)(128)(4,1)}), s8[4194304]{0:T(1024)(128)(4,1)S(1)}, s32[]{:S(2)}) async-start(s8[8388608]{0:T(1024)(128)(4,1)} %bitcast.340), calls=%async_computation.6 | async-start | bytes 8388608 | tf_op jit(solution)/shard_map/while
  389.8 5.0 slice-start.1
  398.5 3.5 copy-start.5
  402.0 4.6 copy-start.16
  487.7 4.7 copy-start.2
  487.7 5.1 copy-start.3
  504.6 9.5 %slice-start = ((s8[8388608]{0:T(1024)(128)(4,1)}), s8[4194304]{0:T(1024)(128)(4,1)S(1)}, s32[]{:S(2)}) async-start(s8[8388608]{0:T(1024)(128)(4,1)} %bitcast.340), calls=%async_computation.6 | async-start | bytes 8388608 | tf_op jit(solution)/shard_map/while
  509.1 5.0 slice-start.1
  517.8 3.5 copy-start.5
  521.3 4.6 copy-start.16
  622.4 9.6 %copy-start.38 = (f32[1024]{0:T(1024)S(1)}, f32[1024]{0:T(1024)}, u32[]{:S(2)}) copy-start(f32[1024]{0:T(1024)} %copy-done.37) | copy-start | bytes 12292
  622.4 9.6 %copy-start.42 = (f32[1024]{0:T(1024)S(1)}, f32[1024]{0:T(1024)}, u32[]{:S(2)}) copy-start(f32[1024]{0:T(1024)} %copy-done.41) | copy-start | bytes 12292
  633.9 17.4 %copy-start.47 = (f32[1024]{0:T(1024)S(1)}, f32[1024]{0:T(1024)}, u32[]{:S(2)}) copy-start(f32[1024]{0:T(1024)} %copy-done.46) | copy-start | bytes 12292
  658.1 44.1 %copy-start.28 = (bf16[800,512]{1,0:T(8,128)(2,1)S(1)}, bf16[800,512]{1,0:T(8,128)(2,1)}, u32[]{:S(2)}) copy-start(bf16[800,512]{1,0:T(8,128)(2,1)} %param.76) | copy-start | bytes 2457604
  658.1 44.5 %copy-start.32 = (f32[10,800]{1,0:T(8,128)S(1)}, f32[10,800]{1,0:T(8,128)}, u32[]{:S(2)}) copy-start(f32[10,800]{1,0:T(8,128)} %copy-done.31) | copy-start | bytes 96004
  662.1 54.7 %copy-start.34 = (bf16[10,1024]{1,0:T(8,128)(2,1)S(1)}, bf16[10,1024]{1,0:T(8,128)(2,1)}, u32[]{:S(2)}) copy-start(bf16[10,1024]{1,0:T(8,128)(2,1)} %param.73) | copy-start | bytes 61444
  (42 other events, 93.9 us)
Sparse Core Ops, SparseCore 0:
  10.9 72.1 all-gather.4
  86.0 54.9 all-gather.6
  143.8 76.3 all-gather.8
  223.0 76.1 all-gather.10
  617.4 18.0 reduce-scatter.1
where the time goes:
time: 734 us; the launch traced here: 726 us
  matrix products  349 us (48%)
  other arithmetic  111 us (15%)
  local copies, waits for them, and re-layouts  77.3 us (11%)
  waiting for transfers between devices  72 us (10%)
  blocking collectives  52.8 us (7%)
  loops' own time  49.1 us (7%)
  between operations  14.5 us (2%)
    dot_general x16, matrix products, block_scores(): jnp.einsum('qgd,kgd->gqk', q_block, keys, preferred_element_type=jnp.floa...  75.9 us
    dot_general x8, matrix products, one_block(): jnp.einsum('qgd,kgd->gqk', g_block[:, head_part], values[:, head_part], p...  75.1 us
    convert_element_type x2, other arithmetic, one_block(): grad_scores = (attn_probs * (grad_probs - row_dot)).astype(jnp.bfloat16)  55.6 us
    dot_general x5, matrix products, back_dot(): lax.dot_general(grad, weight, (((1,), (1,)), ((), ())), preferred_element...  44.9 us
    all_gather x1, waiting for transfers between devices, per_device(): lax.all_gather(qkv_weight, ('rows', 'pre'), axis=0, tiled=True)  41.4 us
    psum x1, blocking collectives, per_device(): summed = lax.psum(prefix_grad.astype(jnp.bfloat16), 'rows')  35.6 us
    another operation x1, loops' own time, attend_backward(): lax.scan(one_block, (token_zeros, token_zeros, prefix_zeros, prefix_zeros...  33.4 us
    all_gather x1, waiting for transfers between devices, per_device(): lax.all_gather(out_weight, ('rows', 'pre'), axis=0, tiled=True)  28 us
  transfers between devices with their start and end apart: 5, of which 2 were waited for; matrix products, arithmetic and copies ran while one was open for 33% of the time, Pallas kernels for 0%

commit v1 on v0

v1 whole, which is shorter than its diff:
```python
import functools

import jax
import jax.numpy as jnp
from jax import lax
from jax.experimental import pallas as pl
from jax.experimental.pallas import tpu as pltpu
from jax.sharding import PartitionSpec as P

f32 = jnp.float32
bf16 = jnp.bfloat16
ALL = ("rows", "pre")
NEG = -1e30
EPS = 1e-05
HD = 64
SPAN = 256
BQ = SPAN
PW = 16
LANES = 256
HEADS = LANES // HD
GROUPS = 2
CHUNKS = 4
BM = 256

NN = (((1,), (0,)), ((), ()))
NT = (((1,), (1,)), ((), ()))
TN = (((0,), (0,)), ((), ()))


def dot(a, b, dims=NN):
    return lax.dot_general(a, b, dims, preferred_element_type=f32)


def params():
    return pltpu.CompilerParams(vmem_limit_bytes=56 << 20)


def cost(flops, moved):
    return pl.CostEstimate(flops=int(flops), bytes_accessed=int(moved), transcendentals=0)


class Weight:
    def __init__(self, arrays, block, table, rows):
        self.arrays, self.block, self.table, self.rows = arrays, block, table, rows
        self.cols = arrays[0].shape[1]

    def specs(self):
        return [pl.BlockSpec(memory_space=pltpu.SMEM)] + [
            pl.BlockSpec(memory_space=pl.ANY) for _ in self.arrays
        ]

    def args(self):
        return [self.table] + list(self.arrays)

    def count(self):
        return 1 + len(self.arrays)

    def scratch(self):
        return [pltpu.VMEM((self.rows, self.cols), bf16), pltpu.SemaphoreType.DMA]


def start_load(refs, block, whole, sem):
    table, arrays = refs[0], refs[1:]
    at = 0
    for ref in arrays:
        for k in range(ref.shape[0] // block):
            first = pl.multiple_of(table[at], block)
            pltpu.make_async_copy(
                ref.at[pl.ds(k * block, block)], whole.at[pl.ds(first, block)], sem
            ).start()
            at += 1


def wait_load(whole, sem):
    pltpu.make_async_copy(whole, whole, sem).wait()


def split(refs, *counts):
    out, at = [], 0
    for n in counts:
        out.append(refs[at : at + n])
        at += n
    return out


def norm(values):
    center = values - jnp.mean(values, axis=-1, keepdims=True)
    rate = lax.rsqrt(jnp.mean(center * center, axis=-1, keepdims=True) + EPS)
    return center * rate, rate


def norm_back(values, gain, grad):
    n, rate = norm(values)
    w = grad * gain
    return rate * (
        w - jnp.mean(w, axis=-1, keepdims=True) - n * jnp.mean(w * n, axis=-1, keepdims=True)
    )


def rows_spec(cols, at=0):
    return pl.BlockSpec((BM, cols), lambda i: (i, at))


def whole_spec(shape):
    return pl.BlockSpec(shape, lambda i: (0,) * len(shape))


def project_kernel(w, *refs):
    x_ref, b_ref, wr, (o_ref, whole, sem) = *refs[:2], refs[2 : 2 + w.count()], refs[2 + w.count() :]

    @pl.when(pl.program_id(0) == 0)
    def _():
        start_load(wr, w.block, whole, sem)
        wait_load(whole, sem)

    o_ref[...] = (dot(x_ref[...], whole[...]) + b_ref[...]).astype(bf16)


def project(x, w, bias):
    length = x.shape[0]
    return pl.pallas_call(
        functools.partial(project_kernel, w),
        grid=(length // BM,),
        in_specs=[rows_spec(w.rows), whole_spec((1, w.cols))] + w.specs(),
        out_specs=rows_spec(w.cols),
        out_shape=jax.ShapeDtypeStruct((length, w.cols), bf16),
        scratch_shapes=w.scratch(),
        compiler_params=params(),
        cost_estimate=cost(2 * length * w.rows * w.cols, 2 * w.rows * w.cols + 4 * length * w.cols),
        name="project",
    )(x, bias, *w.args())


def middle_kernel(w, *refs):
    head = refs[: GROUPS + 4]
    parts, (x_ref, b_ref, g_ref, s_ref) = head[:GROUPS], head[GROUPS:]
    wr = refs[GROUPS + 4 : GROUPS + 4 + w.count()]
    mid_ref, n_ref, whole, sem = refs[GROUPS + 4 + w.count() :]

    @pl.when(pl.program_id(0) == 0)
    def _():
        start_load(wr, w.block, whole, sem)
        wait_load(whole, sem)

    attn = jnp.concatenate([p[...] for p in parts], 1)
    mid = x_ref[...].astype(f32) + (dot(attn, whole[...]) + b_ref[...])
    mid_ref[...] = mid
    n_ref[...] = (norm(mid)[0] * g_ref[...] + s_ref[...]).astype(bf16)


def middle_block(parts, x, w, bias, gain, shift):
    length, model = x.shape
    vec = whole_spec((1, model))
    return pl.pallas_call(
        functools.partial(middle_kernel, w),
        grid=(length // BM,),
        in_specs=[rows_spec(p.shape[1]) for p in parts] + [rows_spec(model), vec, vec, vec] + w.specs(),
        out_specs=[rows_spec(model)] * 2,
        out_shape=[
            jax.ShapeDtypeStruct((length, model), f32),
            jax.ShapeDtypeStruct((length, model), bf16),
        ],
        scratch_shapes=w.scratch(),
        compiler_params=params(),
        cost_estimate=cost(2 * length * w.rows * w.cols, 12 * length * model),
        name="middle_block",
    )(*parts, x, bias, gain, shift, *w.args())


def gelu_both(v):
    c, a = 0.7978845608, 0.044715
    sq = v * v
    t = jnp.tanh(v * (c + (c * a) * sq))
    half = 0.5 + 0.5 * t
    act = v * half
    slope = half + (0.5 * v) * (1.0 - t * t) * (c + (3.0 * c * a) * sq)
    return act, slope


def expand_kernel(w, *refs):
    x_ref, b_ref, wr = refs[0], refs[1], refs[2 : 2 + w.count()]
    act_ref, slope_ref, whole, sem = refs[2 + w.count() :]

    @pl.when(pl.program_id(0) == 0)
    def _():
        start_load(wr, w.block, whole, sem)
        wait_load(whole, sem)

    step = 512
    for j in range(0, w.cols, step):
        at = pl.ds(j, step)
        act, slope = gelu_both(dot(x_ref[...], whole[:, at]) + b_ref[:, at])
        act_ref[:, at] = act.astype(bf16)
        slope_ref[:, at] = slope.astype(bf16)


def expand(x, w, bias):
    length = x.shape[0]
    return pl.pallas_call(
        functools.partial(expand_kernel, w),
        grid=(length // BM,),
        in_specs=[rows_spec(w.rows), whole_spec((1, w.cols))] + w.specs(),
        out_specs=[rows_spec(w.cols)] * 2,
        out_shape=[jax.ShapeDtypeStruct((length, w.cols), bf16)] * 2,
        scratch_shapes=w.scratch(),
        compiler_params=params(),
        cost_estimate=cost(2 * length * w.rows * w.cols, 2 * w.rows * w.cols + 4 * length * w.cols),
        name="expand",
    )(x, bias, *w.args())


def contract_kernel(w_in, w_out, w_proj, chunk, first, last, *refs):
    refs = list(refs)
    og_ref, act_ref, slope_ref, mid_ref = refs[:4]
    refs = refs[4:]
    if first:
        ob_ref = refs.pop(0)
    else:
        out_in, gn_in = refs.pop(0), refs.pop(0)
    if last:
        g_ref = refs.pop(0)
    wi, refs = refs[: w_in.count()], refs[w_in.count() :]
    wo, refs = refs[: w_out.count()], refs[w_out.count() :]
    if last:
        wp, refs = refs[: w_proj.count()], refs[w_proj.count() :]
        out_ref, gm_ref, ga_ref = refs[:3]
        refs = refs[3:]
    else:
        out_ref, gn_ref = refs[:2]
        refs = refs[2:]
    fc, fc_sem, ow, ow_sem = refs[:4]
    width = w_out.rows

    @pl.when(pl.program_id(0) == 0)
    def _():
        start_load(wo, w_out.block, ow, ow_sem)
        table, arrays = wi[0], wi[1:]
        at = 0
        for ref in arrays:
            for k in range(ref.shape[0] // w_in.block):
                row = pl.multiple_of(table[at], w_in.block)
                pltpu.make_async_copy(
                    ref.at[pl.ds(k * w_in.block, w_in.block), pl.ds(chunk * width, width)],
                    fc.at[pl.ds(row, w_in.block)],
                    fc_sem,
                ).start()
                at += 1
        if last:
            start_load(wp, w_proj.block, refs[4], refs[5])
            wait_load(refs[4], refs[5])
        wait_load(ow, ow_sem)
        wait_load(fc, fc_sem)

    og = og_ref[...]
    grad_act = dot(og, ow[...], NT)
    grad_pre = (grad_act * slope_ref[...].astype(f32)).astype(bf16)
    gn = dot(grad_pre, fc[...], NT)
    out = dot(act_ref[...], ow[...])
    if first:
        out = out + (mid_ref[...] + ob_ref[...])
    else:
        out = out + out_in[...]
        gn = gn + gn_in[...]
    out_ref[...] = out.astype(out_ref.dtype)
    if last:
        gm = og.astype(f32) + norm_back(mid_ref[...], g_ref[...], gn)
        gm_ref[...] = gm
        ga_ref[...] = dot(gm.astype(bf16), refs[4][...], NT).astype(bf16)
    else:
        gn_ref[...] = gn


def contract(chunk, og, act, slope, mid, out_bias, gain, so_far, w_in, w_out, w_proj):
    length, model = og.shape
    first, last = chunk == 0, chunk == CHUNKS - 1
    width = w_out.rows
    vec = whole_spec((1, model))
    full = rows_spec(model)
    specs = [full, rows_spec(width, chunk), rows_spec(width, chunk), full]
    args = [og, act, slope, mid]
    if first:
        specs, args = specs + [vec], args + [out_bias]
    else:
        specs, args = specs + [full, full], args + list(so_far)
    if last:
        specs, args = specs + [vec], args + [gain]
    specs, args = specs + w_in.specs() + w_out.specs(), args + w_in.args() + w_out.args()
    scratch = [pltpu.VMEM((w_in.rows, width), bf16), pltpu.SemaphoreType.DMA] + w_out.scratch()
    if last:
        specs, args = specs + w_proj.specs(), args + w_proj.args()
        scratch = scratch + w_proj.scratch()
        outs = [bf16, f32, bf16]
    else:
        outs = [f32, f32]
    return pl.pallas_call(
        functools.partial(contract_kernel, w_in, w_out, w_proj, chunk, first, last),
        grid=(length // BM,),
        in_specs=specs,
        out_specs=[full] * len(outs),
        out_shape=[jax.ShapeDtypeStruct((length, model), t) for t in outs],
        scratch_shapes=scratch,
        compiler_params=params(),
        cost_estimate=cost(6 * length * width * model, 24 * length * model),
        name="contract",
    )(*args)


def finish_kernel(ws, *refs):
    n = 3 * GROUPS
    parts, refs = refs[:n], refs[n:]
    (x_ref, gm_ref, g_ref), refs = refs[:3], refs[3:]
    wr = []
    for w in ws:
        wr.append(refs[: w.count()])
        refs = refs[w.count() :]
    o_ref, scratch = refs[0], refs[1:]

    @pl.when(pl.program_id(0) == 0)
    def _():
        for i, w in enumerate(ws):
            start_load(wr[i], w.block, scratch[2 * i], scratch[2 * i + 1])
        for i in range(len(ws)):
            wait_load(scratch[2 * i], scratch[2 * i + 1])

    gn = 0.0
    for i in range(GROUPS):
        part = jnp.concatenate([r[...] for r in parts[3 * i : 3 * i + 3]], 1)
        gn = gn + dot(part, scratch[2 * i][...], NT)
    o_ref[...] = (gm_ref[...] + norm_back(x_ref[...].astype(f32), g_ref[...], gn)).astype(bf16)


def finish(parts, x, gm, gain, ws):
    length, model = x.shape
    full = rows_spec(model)
    return pl.pallas_call(
        functools.partial(finish_kernel, ws),
        grid=(length // BM,),
        in_specs=[rows_spec(p.shape[1]) for p in parts]
        + [full, full, whole_spec((1, model))]
        + sum([w.specs() for w in ws], []),
        out_specs=full,
        out_shape=jax.ShapeDtypeStruct((length, model), bf16),
        scratch_shapes=sum([w.scratch() for w in ws], []),
        compiler_params=params(),
        cost_estimate=cost(6 * length * model * model, 16 * length * model),
        name="finish",
    )(*parts, x, gm, gain, *sum([w.args() for w in ws], []))


def spans(length):
    out, at = [], 0
    for first in range(0, length, BQ):
        key = max(0, first - SPAN)
        keys = PW + first + BQ - key
        out.append((first, key, keys, at))
        at += keys
    return out, at


def mask_bias(seg, valid, prefix):
    length = seg.shape[0]
    place = jnp.arange(length)
    parts = []
    for first, key, keys, _ in spans(length)[0]:
        ks, qs = slice(key, key + keys - PW), slice(first, first + BQ)
        seen = (
            (seg[ks][:, None] == seg[qs][None, :])
            & (place[ks][:, None] <= place[qs][None, :])
            & (valid[ks][:, None] > 0)
        )
        pad = jnp.broadcast_to(jnp.arange(PW)[:, None] < prefix, (PW, BQ))
        parts += [pad, seen]
    return jnp.where(jnp.concatenate(parts, 0), 0.0, NEG).astype(f32)


def of_head(shape, head):
    lane = lax.broadcasted_iota(jnp.int32, shape, 1)
    return (lane >= HD * head) & (lane < HD * (head + 1))


def stack_heads(q):
    return jnp.concatenate([jnp.where(of_head(q.shape, h), q, jnp.zeros_like(q)) for h in range(HEADS)], 0)


def pick_heads(o):
    out = o[:BQ]
    for h in range(1, HEADS):
        out = jnp.where(of_head(out.shape, h), o[h * BQ : (h + 1) * BQ], out)
    return out


def attend_kernel(length, q_ref, k_ref, v_ref, pk_ref, pv_ref, bias_ref, o_ref, p_ref):
    plan = spans(length)[0]

    def score(i):
        first, key, keys, _ = plan[i]
        q = q_ref[pl.ds(first, BQ), :] * jnp.asarray(HD**-0.5, bf16)
        ks = jnp.concatenate([pk_ref[...], k_ref[pl.ds(key, keys - PW), :]], 0)
        return dot(ks, stack_heads(q), NT)

    def soft(i, s):
        _, _, keys, at = plan[i]
        s = s + jnp.concatenate([bias_ref[pl.ds(at, keys), :]] * HEADS, 1)
        e = jnp.exp(s - jnp.max(s, axis=0, keepdims=True))
        probs = (e * (1.0 / jnp.sum(e, axis=0, keepdims=True))).astype(bf16)
        p_ref[0, pl.ds(at, keys), :] = probs
        return probs

    def mix(i, probs):
        first, key, keys, _ = plan[i]
        vs = jnp.concatenate([pv_ref[...], v_ref[pl.ds(key, keys - PW), :]], 0)
        o_ref[pl.ds(first, BQ), :] = pick_heads(dot(probs, vs, TN)).astype(bf16)

    n = len(plan)
    s, held = score(0), None
    for i in range(n):
        later = score(i + 1) if i + 1 < n else None
        probs = soft(i, s)
        if held is not None:
            mix(i - 1, held)
        s, held = later, probs
    mix(n - 1, held)


def attend(qkv, pk, pv, bias):
    length = qkv.shape[0]
    steps = qkv.shape[1] // 3 // LANES
    total = spans(length)[1]

    def col(at):
        return pl.BlockSpec((length, LANES), lambda i: (0, at * steps + i))

    small = pl.BlockSpec((PW, LANES), lambda i: (0, i))
    return pl.pallas_call(
        functools.partial(attend_kernel, length),
        grid=(steps,),
        in_specs=[col(0), col(1), col(2), small, small, whole_spec((total, BQ))],
        out_specs=[col(0), pl.BlockSpec((1, total, HEADS * BQ), lambda i: (i, 0, 0))],
        out_shape=[
            jax.ShapeDtypeStruct((length, steps * LANES), bf16),
            jax.ShapeDtypeStruct((steps, total, HEADS * BQ), bf16),
        ],
        compiler_params=params(),
        cost_estimate=cost(steps * 5e9, steps * 6e6),
        name="attend",
    )(qkv, qkv, qkv, pk, pv, bias)


def attend_back_kernel(
    length, q_ref, k_ref, v_ref, pk_ref, pv_ref, p_ref, do_ref, dq_ref, dk_ref, dv_ref, dpk_ref, dpv_ref, ak, av
):
    ak[...] = jnp.zeros_like(ak)
    av[...] = jnp.zeros_like(av)
    for first, key, keys, at in spans(length)[0]:
        n = keys - PW
        qs = stack_heads(q_ref[pl.ds(first, BQ), :] * jnp.asarray(HD**-0.5, bf16))
        dos = stack_heads(do_ref[pl.ds(first, BQ), :])
        ks = jnp.concatenate([pk_ref[...], k_ref[pl.ds(key, n), :]], 0)
        vs = jnp.concatenate([pv_ref[...], v_ref[pl.ds(key, n), :]], 0)
        dp = dot(vs, dos, NT)
        probs = p_ref[0, pl.ds(at, keys), :]
        wide = probs.astype(f32)
        t = wide * dp
        ds = (t - wide * jnp.sum(t, axis=0, keepdims=True)).astype(bf16)
        dk = dot(ds, qs)
        dv = dot(probs, dos)
        dq_ref[pl.ds(first, BQ), :] = (pick_heads(dot(ds, ks, TN)) * HD**-0.5).astype(bf16)
        ak[pl.ds(0, PW), :] += dk[:PW]
        av[pl.ds(0, PW), :] += dv[:PW]
        ak[pl.ds(PW + key, n), :] += dk[PW:]
        av[pl.ds(PW + key, n), :] += dv[PW:]
    dpk_ref[...] = ak[pl.ds(0, PW), :]
    dpv_ref[...] = av[pl.ds(0, PW), :]
    dk_ref[...] = ak[pl.ds(PW, length), :].astype(bf16)
    dv_ref[...] = av[pl.ds(PW, length), :].astype(bf16)


def attend_back(group, qkv, pk, pv, probs, do):
    length = qkv.shape[0]
    steps = qkv.shape[1] // 3 // LANES
    total = spans(length)[1]

    def col(at):
        return pl.BlockSpec((length, LANES), lambda i: (0, at * steps + i))

    small = pl.BlockSpec((PW, LANES), lambda i: (0, i))
    return pl.pallas_call(
        functools.partial(attend_back_kernel, length),
        grid=(steps,),
        in_specs=[col(0), col(1), col(2), small, small]
        + [pl.BlockSpec((1, total, HEADS * BQ), lambda i: (i, 0, 0)), col(group)],
        out_specs=[col(0)] * 3 + [small] * 2,
        out_shape=[jax.ShapeDtypeStruct((length, steps * LANES), bf16)] * 3
        + [jax.ShapeDtypeStruct((PW, steps * LANES), f32)] * 2,
        scratch_shapes=[pltpu.VMEM((PW + length, LANES), f32)] * 2,
        compiler_params=params(),
        cost_estimate=cost(steps * 6e9, steps * 8e6),
        name="attend_back",
    )(qkv, qkv, qkv, pk, pv, probs, do)


def gather_plain(shard):
    whole = lax.all_gather(shard, ALL, axis=0, tiled=True)
    return Weight([whole], whole.shape[0], jnp.zeros((1,), jnp.int32), whole.shape[0])


def per_device(
    tokens,
    seg_ids,
    valid,
    out_grad,
    ln1_gain,
    ln1_bias,
    qkv_weight,
    qkv_bias,
    proj_weight,
    proj_bias,
    ln2_gain,
    ln2_bias,
    fc_weight,
    fc_bias,
    out_weight,
    out_bias,
    prefix_emb,
    rep_weight1,
    rep_bias1,
    rep_weight2,
    rep_bias2,
):
    x, og = tokens[0], out_grad[0]
    length, model = x.shape
    devices = lax.axis_size(ALL)
    hidden_units = fc_weight.shape[1]
    prefix_len = prefix_emb.shape[0]
    gather = gather_plain

    def vec(a):
        return a.astype(f32).reshape(1, -1)

    part = model // GROUPS
    qkv_parts = [
        jnp.concatenate([qkv_weight[:, i * model + g * part : i * model + (g + 1) * part] for i in range(3)], 1)
        for g in range(GROUPS)
    ]
    qkv_biases = [
        jnp.concatenate([qkv_bias[i * model + g * part : i * model + (g + 1) * part] for i in range(3)])
        for g in range(GROUPS)
    ]
    own = out_weight.shape[0] // CHUNKS

    def regroup(a):
        lead = a.shape[:-1]
        a = a.reshape(lead + (devices, CHUNKS, own))
        return jnp.swapaxes(a, -2, -3).reshape(lead + (hidden_units,))

    fc_shard, fc_shift = regroup(fc_weight), regroup(fc_bias)

    pre_hidden = jnp.dot(prefix_emb, rep_weight1, preferred_element_type=f32) + rep_bias1.astype(f32)
    hidden = jnp.tanh(pre_hidden)
    hidden_low = hidden.astype(bf16)
    kv_local = (jnp.dot(hidden_low, rep_weight2, preferred_element_type=f32) + rep_bias2.astype(f32)).astype(bf16)
    prefix_kv = lax.all_gather(kv_local, "pre", axis=1, tiled=True)
    prefix_kv = jnp.pad(prefix_kv, ((0, PW - prefix_len), (0, 0)))

    w_qkv = [gather(p) for p in qkv_parts]
    w_proj = gather(proj_weight)
    w_fc = gather(fc_shard)
    w_out = [gather(out_weight[j * own : (j + 1) * own]) for j in range(CHUNKS)]

    bias = mask_bias(seg_ids[0], valid[0], prefix_len)
    xf = x.astype(f32)
    normed1 = (norm(xf)[0] * ln1_gain.astype(f32) + ln1_bias.astype(f32)).astype(bf16)

    qkvs, mixes, probs, pks, pvs = [], [], [], [], []
    for g in range(GROUPS):
        pks.append(prefix_kv[:, g * part : (g + 1) * part])
        pvs.append(prefix_kv[:, model + g * part : model + (g + 1) * part])
        qkvs.append(project(normed1, w_qkv[g], vec(qkv_biases[g])))
        o, p = attend(qkvs[g], pks[g], pvs[g], bias)
        mixes.append(o)
        probs.append(p)
    mid, normed2 = middle_block(mixes, x, w_proj, vec(proj_bias), vec(ln2_gain), vec(ln2_bias))
    act, slope = expand(normed2, w_fc, vec(fc_shift))
    so_far = None
    for j in range(CHUNKS):
        so_far = contract(j, og, act, slope, mid, vec(out_bias), vec(ln2_gain), so_far, w_fc, w_out[j], w_proj)
    output, grad_mid, grad_attn = so_far

    parts, dpk, dpv = [], [], []
    for g in range(GROUPS):
        dq, dk, dv, a, b = attend_back(g, qkvs[g], pks[g], pvs[g], probs[g], grad_attn)
        parts += [dq, dk, dv]
        dpk.append(a)
        dpv.append(b)
    in_grad = finish(parts, x, grad_mid, vec(ln1_gain), w_qkv)

    prefix_grad = jnp.concatenate(dpk + dpv, 1)[:prefix_len]
    summed = lax.psum(prefix_grad.astype(bf16), "rows")
    kv_low = lax.psum_scatter(summed, "pre", scatter_dimension=1, tiled=True)
    bias2_grad = jnp.sum(kv_low.astype(f32), axis=0)
    weight2_grad = dot(hidden_low, kv_low, TN)
    hid_grad = lax.psum(dot(kv_low, rep_weight2, NT), "pre")
    pre_grad = (hid_grad * (1.0 - hidden * hidden)).astype(bf16)
    bias1_grad = jnp.sum(pre_grad.astype(f32), axis=0)
    weight1_grad = dot(prefix_emb, pre_grad, TN)
    emb_grad = dot(pre_grad, rep_weight1, NT)
    return output[None], in_grad[None], emb_grad, weight1_grad, bias1_grad, weight2_grad, bias2_grad


def solution(mesh):
    split_all = P(ALL, None)
    whole = P()
    return jax.shard_map(
        per_device,
        mesh=mesh,
        in_specs=(
            P(ALL, None, None),
            split_all,
            split_all,
            P(ALL, None, None),
            whole,
            whole,
            split_all,
            whole,
            split_all,
            whole,
            whole,
            whole,
            split_all,
            whole,
            split_all,
            whole,
            whole,
            whole,
            whole,
            P(None, "pre"),
            P("pre"),
        ),
        out_specs=(
            P(ALL, None, None),
            P(ALL, None, None),
            whole,
            whole,
            whole,
            P(None, "pre"),
            P("pre"),
        ),
        check_vma=False,
    )
```

time: 734 us -> 641 us (0.87)
  matrix products: 349 us -> 5.94 us
  waiting for transfers between devices: 72 us -> 354 us
  Pallas kernels: 0 us -> 179 us
  other arithmetic: 111 us -> 17.2 us
  local copies, waits for them, and re-layouts: 77.3 us -> 9.61 us
  loops' own time: 49.1 us -> 0 us
    dot_general x125 -> x6, matrix products: 349 us -> 5.94 us  [the longest x4 5.18 us: dot(): return lax.dot_general(a, b, dims, preferred_element_type=f32)]
    all_gather x4 -> x8, waiting for transfers between devices: 69.4 us -> 347 us  [gather_plain(): whole = lax.all_gather(shard, ALL, axis=0, tiled=True)]
    pallas_call x0 -> x13, Pallas kernels: none -> 179 us  [the longest x4 61.4 us: contract(): pl.pallas_call(functools.partial(contract_kernel, w_in, w_out, w_proj, ch...]
    convert_element_type x20 -> x7, other arithmetic: 65.6 us -> 4.95 us  [the longest x1 3.73 us: per_device(): (norm(xf)[0] * ln1_gain.astype(f32) + ln1_bias.astype(f32)).astype(bf16)]
    another operation x2 -> x0, loops' own time: 49.1 us -> none  [the longest x1 33.4 us: attend_backward(): lax.scan(one_block, (token_zeros, token_zeros, prefix_zeros, prefix_zeros...]
    reduce_sum x17 -> x4, other arithmetic: 31.9 us -> 2.25 us  [the longest x1 0.69 us: norm(): rate = lax.rsqrt(jnp.mean(center * center, axis=-1, keepdims=True) + EPS)]
    unnamed x68 -> x40, local copies, waits for them, and re-layouts: 25.1 us -> 0.42 us
    while x110 -> x0, local copies, waits for them, and re-layouts: 18.7 us -> none
  transfers between devices with their start and end apart: 5 -> 9, of which waited for: 2 -> 9; matrix products, arithmetic and copies ran while one was open for 33% -> 3% of each run, Pallas kernels for 0% -> 21%
where the time goes in v1:
time: 641 us; the launch traced here: 635 us
  waiting for transfers between devices  354 us (55%)
  Pallas kernels  179 us (28%)
  blocking collectives  54.4 us (8%)
  other arithmetic  17.2 us (3%)
  between operations  14.6 us (2%)
  local copies, waits for them, and re-layouts  9.61 us (1%)
    all_gather x8, waiting for transfers between devices, gather_plain(): whole = lax.all_gather(shard, ALL, axis=0, tiled=True)  347 us
    pallas_call x4, Pallas kernels, contract(): pl.pallas_call(functools.partial(contract_kernel, w_in, w_out, w_proj, ch...  61.4 us
    psum x1, blocking collectives, per_device(): summed = lax.psum(prefix_grad.astype(bf16), 'rows')  37.1 us
    pallas_call x2, Pallas kernels, attend_back(): pl.pallas_call(functools.partial(attend_back_kernel, length), grid=(steps...  29.7 us
    pallas_call x1, Pallas kernels, expand(): pl.pallas_call(functools.partial(expand_kernel, w), grid=(length // BM,),...  24.8 us
    pallas_call x2, Pallas kernels, attend(): pl.pallas_call(functools.partial(attend_kernel, length), grid=(steps,), i...  24.2 us
    pallas_call x2, Pallas kernels, project(): pl.pallas_call(functools.partial(project_kernel, w), grid=(length // BM,)...  16.4 us
    pallas_call x1, Pallas kernels, finish(): pl.pallas_call(functools.partial(finish_kernel, ws), grid=(length // BM,)...  14.4 us
  transfers between devices with their start and end apart: 9, of which 9 were waited for; matrix products, arithmetic and copies ran while one was open for 3% of the time, Pallas kernels for 21%

profile of v1, /device:TPU:0, one launch (start us, length us, event | category | flops | bytes accessed | tf_op | source)
XLA Modules:
  0.0 635.0 jit_solution(3618068037605987513)
XLA Ops:
  7.2 1.0 fusion.12
  8.2 0.7 pad_maximum_fusion.1
  9.0 0.6 pad_maximum_fusion
  9.7 0.7 all-gather.13.cloned.1.call-update
  10.5 2.7 reshape.243
  13.1 1.4 copy.32
  14.6 1.9 reshape.244
  16.6 0.7 fusion.11
  17.9 0.7 all-gather.21.cloned.1.call-update
  18.6 0.7 all-gather.23.cloned.1.call-update
  21.2 1.5 broadcast_select_fusion.bias_ref
  23.1 0.7 fusion.2
  24.7 6.4 %all_gather.28 = bf16[10,2048]{1,0:T(8,128)(2,1)S(1)} all-gather(bf16[10,512]{1,0:T(8,128)(2,1)S(1)} %fusion.7), channel_id=1, replica_groups=mesh['rows'=8,'pre'=4] {'pre'}, dimensions={1}, use_global_device_ids=true | all-gather | bytes 51200 | tf_op jit(solution)/shard_map/all_gather | solution.py:562
  31.1 0.6 pad_slice_fusion
  33.7 0.7 reshape.253.refs_1_
  35.6 3.7 fusion.5.refs_0_
  39.9 32.8 %all-gather.11.cloned.1.call-done.refs_3_.refs_12_ = bf16[1024,1536]{1,0:T(8,128)(2,1)} async-done(((bf16[32,1536]{1,0:T(8,128)(2,1)}), bf16[1024,1536]{1,0:T(8,128)(2,1)}) %all-gather.11.cloned.1.call-update) | async-done | bytes 3145744 | tf_op jit(solution)/shard_map/all_gather | solution.py:503
  72.7 8.2 %project.3.q_ref.k_ref.v_ref = bf16[1024,1536]{1,0:T(8,128)(2,1)} custom-call(bf16[1024,1024]{1,0:T(8,128)(2,1)} %fusion.5.refs_0_, f32[1,1536]{1,0:T(1,128)} %maximum_convert_fusion.1.refs_1_, s32[1]{0:T(128)} %constant.5.clone.1.refs_2_.refs_6_.refs_5_.refs_7_.refs_8_.refs_9_.refs_11_, bf16[1024,1536]{1,0:T(8,128)(2,1)} %all-gather.11.cloned.1.call-done.refs_3_.refs_12_), custom_call_target="tpu_custom_call" | custom-call | flops 3221225472 | bytes 9437184 | tf_op jit(solution)/shard_map/project/pallas_call | solution.py:121
  80.9 12.1 %attend.3 = (bf16[1024,512]{1,0:T(8,128)(2,1)}, bf16[2,1856,1024]{2,1,0:T(8,128)(2,1)}) custom-call(bf16[1024,1536]{1,0:T(8,128)(2,1)} %project.3.q_ref.k_ref.v_ref, bf16[1024,1536]{1,0:T(8,128)(2,1)} %project.3.q_ref.k_ref.v_ref, bf16[1024,1536]{1,0:T(8,128)(2,1)} %project.3.q_ref.k_ref.v_ref, bf16[16,512]{1,0:T(8,128)(2,1)} %get-tuple-element.78.pk_ref, ...), custom_call_target="tpu_custom_call" | custom-call | flops 10000000000 | bytes 12000000 | tf_op jit(solution)/shard_map/attend/pallas_call | solution.py:434
  93.0 41.0 %all-gather.9.cloned.1.call-done.refs_3_.refs_10_ = bf16[1024,1536]{1,0:T(8,128)(2,1)} async-done(((bf16[32,1536]{1,0:T(8,128)(2,1)}), bf16[1024,1536]{1,0:T(8,128)(2,1)}) %all-gather.9.cloned.1.call-update) | async-done | bytes 3145744 | tf_op jit(solution)/shard_map/all_gather | solution.py:503
  134.1 8.2 %project.2.q_ref.k_ref.v_ref = bf16[1024,1536]{1,0:T(8,128)(2,1)} custom-call(bf16[1024,1024]{1,0:T(8,128)(2,1)} %fusion.5.refs_0_, f32[1,1536]{1,0:T(1,128)} %maximum_convert_fusion.refs_1_, s32[1]{0:T(128)} %constant.5.clone.1.refs_2_.refs_6_.refs_5_.refs_7_.refs_8_.refs_9_.refs_11_, bf16[1024,1536]{1,0:T(8,128)(2,1)} %all-gather.9.cloned.1.call-done.refs_3_.refs_10_), custom_call_target="tpu_custom_call" | custom-call | flops 3221225472 | bytes 9437184 | tf_op jit(solution)/shard_map/project/pallas_call | solution.py:121
  142.3 12.1 %attend.2 = (bf16[1024,512]{1,0:T(8,128)(2,1)}, bf16[2,1856,1024]{2,1,0:T(8,128)(2,1)}) custom-call(bf16[1024,1536]{1,0:T(8,128)(2,1)} %project.2.q_ref.k_ref.v_ref, bf16[1024,1536]{1,0:T(8,128)(2,1)} %project.2.q_ref.k_ref.v_ref, bf16[1024,1536]{1,0:T(8,128)(2,1)} %project.2.q_ref.k_ref.v_ref, bf16[16,512]{1,0:T(8,128)(2,1)} %get-tuple-element.79.pk_ref, ...), custom_call_target="tpu_custom_call" | custom-call | flops 10000000000 | bytes 12000000 | tf_op jit(solution)/shard_map/attend/pallas_call | solution.py:434
  154.4 37.8 %all-gather.13.cloned.1.call-done.refs_7_.refs_12_ = bf16[1024,1024]{1,0:T(8,128)(2,1)} async-done(((bf16[32,1024]{1,0:T(8,128)(2,1)}), bf16[1024,1024]{1,0:T(8,128)(2,1)}) %all-gather.13.cloned.1.call-update) | async-done | bytes 2097168 | tf_op jit(solution)/shard_map/all_gather | solution.py:503
  192.2 8.3 %middle_block.1 = (f32[1024,1024]{1,0:T(8,128)}, bf16[1024,1024]{1,0:T(8,128)(2,1)}) custom-call(bf16[1024,512]{1,0:T(8,128)(2,1)} %get-tuple-element.34.refs_0_, bf16[1024,512]{1,0:T(8,128)(2,1)} %get-tuple-element.35.refs_1_, bf16[1024,1024]{1,0:T(8,128)(2,1)} %bitcast.41, f32[1,1024]{1,0:T(1,128)} %bitcast.57, f32[1,1024]{1,0:T(1,128)} %bitcast.46, ...), custom_call_target="tpu_custom_call" | custom-call | flops 2147483648 | bytes 12582912 | tf_op jit(solution)/shard_map/middle_block/pallas_call | solution.py:154
  200.5 70.8 %all-gather.15.cloned.1.call-done.refs_3_.refs_6_.refs_7_.refs_8_ = bf16[1024,4096]{1,0:T(8,128)(2,1)} async-done(((bf16[32,4096]{1,0:T(8,128)(2,1)}), bf16[1024,4096]{1,0:T(8,128)(2,1)}) %all-gather.15.cloned.1.call-update) | async-done | bytes 8388624 | tf_op jit(solution)/shard_map/all_gather | solution.py:503
  271.4 24.8 %expand.1 = (bf16[1024,4096]{1,0:T(8,128)(2,1)}, bf16[1024,4096]{1,0:T(8,128)(2,1)}) custom-call(bf16[1024,1024]{1,0:T(8,128)(2,1)} %get-tuple-element.36.refs_0_, f32[1,4096]{1,0:T(1,128)} %reshape.253.refs_1_, s32[1]{0:T(128)} %constant.5.clone.1.refs_2_.refs_6_.refs_5_.refs_7_.refs_8_.refs_9_.refs_11_, ...), custom_call_target="tpu_custom_call" | custom-call | flops 8589934592 | bytes 25165824 | tf_op jit(solution)/shard_map/expand/pallas_call | solution.py:199
  296.2 32.9 %all-gather.17.cloned.1.call-done.refs_8_ = bf16[1024,1024]{1,0:T(8,128)(2,1)} async-done(((bf16[32,1024]{1,0:T(8,128)(2,1)}), bf16[1024,1024]{1,0:T(8,128)(2,1)}) %all-gather.17.cloned.1.call-update) | async-done | bytes 2097168 | tf_op jit(solution)/shard_map/all_gather | solution.py:503
  329.1 12.9 %contract.4 = (f32[1024,1024]{1,0:T(8,128)}, f32[1024,1024]{1,0:T(8,128)}) custom-call(bf16[1024,1024]{1,0:T(8,128)(2,1)} %bitcast.37, bf16[1024,4096]{1,0:T(8,128)(2,1)} %get-tuple-element.37.refs_1_, bf16[1024,4096]{1,0:T(8,128)(2,1)} %get-tuple-element.38.refs_2_, f32[1024,1024]{1,0:T(8,128)} %get-tuple-element.39.refs_3_, f32[1,1024]{1,0:T(1,128)} %bitcast.48, ...), custom_call_target="tpu_custom_call" | custom-call | flops 6442450944 | bytes 25165824 | tf_op jit(solution)/shard_map/contract/pallas_call | solution.py:295
  342.0 45.1 %all-gather.19.cloned.1.call-done.refs_9_ = bf16[1024,1024]{1,0:T(8,128)(2,1)} async-done(((bf16[32,1024]{1,0:T(8,128)(2,1)}), bf16[1024,1024]{1,0:T(8,128)(2,1)}) %all-gather.19.cloned.1.call-update) | async-done | bytes 2097168 | tf_op jit(solution)/shard_map/all_gather | solution.py:503
  387.1 15.3 %contract.5 = (f32[1024,1024]{1,0:T(8,128)}, f32[1024,1024]{1,0:T(8,128)}) custom-call(bf16[1024,1024]{1,0:T(8,128)(2,1)} %bitcast.38, bf16[1024,4096]{1,0:T(8,128)(2,1)} %get-tuple-element.37.refs_1_, bf16[1024,4096]{1,0:T(8,128)(2,1)} %get-tuple-element.38.refs_2_, f32[1024,1024]{1,0:T(8,128)} %get-tuple-element.39.refs_3_, ...), custom_call_target="tpu_custom_call" | custom-call | flops 6442450944 | bytes 25165824 | tf_op jit(solution)/shard_map/contract/pallas_call | solution.py:295
  402.4 42.9 %all-gather.21.cloned.1.call-done.refs_9_ = bf16[1024,1024]{1,0:T(8,128)(2,1)} async-done(((bf16[32,1024]{1,0:T(8,128)(2,1)}), bf16[1024,1024]{1,0:T(8,128)(2,1)}) %all-gather.21.cloned.1.call-update) | async-done | bytes 2097168 | tf_op jit(solution)/shard_map/all_gather | solution.py:503
  445.3 15.3 %contract.6 = (f32[1024,1024]{1,0:T(8,128)}, f32[1024,1024]{1,0:T(8,128)}) custom-call(bf16[1024,1024]{1,0:T(8,128)(2,1)} %bitcast.39, bf16[1024,4096]{1,0:T(8,128)(2,1)} %get-tuple-element.37.refs_1_, bf16[1024,4096]{1,0:T(8,128)(2,1)} %get-tuple-element.38.refs_2_, f32[1024,1024]{1,0:T(8,128)} %get-tuple-element.39.refs_3_, ...), custom_call_target="tpu_custom_call" | custom-call | flops 6442450944 | bytes 25165824 | tf_op jit(solution)/shard_map/contract/pallas_call | solution.py:295
  460.5 43.4 %all-gather.23.cloned.1.call-done.refs_10_ = bf16[1024,1024]{1,0:T(8,128)(2,1)} async-done(((bf16[32,1024]{1,0:T(8,128)(2,1)}), bf16[1024,1024]{1,0:T(8,128)(2,1)}) %all-gather.23.cloned.1.call-update) | async-done | bytes 2097168 | tf_op jit(solution)/shard_map/all_gather | solution.py:503
  504.0 18.0 %contract.7 = (bf16[1024,1024]{1,0:T(8,128)(2,1)}, f32[1024,1024]{1,0:T(8,128)}, bf16[1024,1024]{1,0:T(8,128)(2,1)}) custom-call(bf16[1024,1024]{1,0:T(8,128)(2,1)} %bitcast.40, bf16[1024,4096]{1,0:T(8,128)(2,1)} %get-tuple-element.37.refs_1_, bf16[1024,4096]{1,0:T(8,128)(2,1)} %get-tuple-element.38.refs_2_, f32[1024,1024]{1,0:T(8,128)} %get-tuple-element.39.refs_3_, ...), custom_call_target="tpu_custom_call" | custom-call | flops 6442450944 | bytes 25165824 | tf_op jit(solution)/shard_map/contract/pallas_call | solution.py:295
  522.0 15.0 %attend_back.3 = (bf16[1024,512]{1,0:T(8,128)(2,1)}, bf16[1024,512]{1,0:T(8,128)(2,1)}, bf16[1024,512]{1,0:T(8,128)(2,1)}, f32[16,512]{1,0:T(8,128)}, f32[16,512]{1,0:T(8,128)}) custom-call(bf16[1024,1536]{1,0:T(8,128)(2,1)} %project.3.q_ref.k_ref.v_ref, bf16[1024,1536]{1,0:T(8,128)(2,1)} %project.3.q_ref.k_ref.v_ref, ...), custom_call_target="tpu_custom_call" | custom-call | flops 12000000000 | bytes 16000000 | tf_op jit(solution)/shard_map/attend_back/pallas_call | solution.py:487
  537.0 0.8 convert.21
  537.7 0.8 convert.23
  538.5 14.7 %attend_back.2 = (bf16[1024,512]{1,0:T(8,128)(2,1)}, bf16[1024,512]{1,0:T(8,128)(2,1)}, bf16[1024,512]{1,0:T(8,128)(2,1)}, f32[16,512]{1,0:T(8,128)}, f32[16,512]{1,0:T(8,128)}) custom-call(bf16[1024,1536]{1,0:T(8,128)(2,1)} %project.2.q_ref.k_ref.v_ref, bf16[1024,1536]{1,0:T(8,128)(2,1)} %project.2.q_ref.k_ref.v_ref, ...), custom_call_target="tpu_custom_call" | custom-call | flops 12000000000 | bytes 16000000 | tf_op jit(solution)/shard_map/attend_back/pallas_call | solution.py:487
  553.2 0.8 convert.20
  554.0 0.8 convert.22
  554.7 0.6 pad_maximum_fusion.2
  555.4 14.4 %finish.1 = bf16[1024,1024]{1,0:T(8,128)(2,1)} custom-call(bf16[1024,512]{1,0:T(8,128)(2,1)} %get-tuple-element.49.refs_0_, bf16[1024,512]{1,0:T(8,128)(2,1)} %get-tuple-element.50.refs_1_, bf16[1024,512]{1,0:T(8,128)(2,1)} %get-tuple-element.51.refs_2_, bf16[1024,512]{1,0:T(8,128)(2,1)} %get-tuple-element.53.refs_3_, ...), custom_call_target="tpu_custom_call" | custom-call | flops 6442450944 | bytes 16777216 | tf_op jit(solution)/shard_map/finish/pallas_call | solution.py:335
  569.8 4.1 reduce-scatter.2.cloned.1.call-done
  573.9 37.1 %psum.16 = bf16[10,512]{1,0:T(8,128)(2,1)S(1)} all-reduce(bf16[10,512]{1,0:T(8,128)(2,1)} %reduce-scatter.2.cloned.1.call-done), channel_id=1, replica_groups=mesh['rows'=8,'pre'=4] {'rows'}, use_global_device_ids=true, to_apply=%region_2.3 | all-reduce | flops 5120 | bytes 20480 | tf_op jit(solution)/shard_map/psum | solution.py:598
  611.2 1.6 fusion.8
  612.8 10.9 %psum.15 = f32[10,800]{1,0:T(8,128)S(1)} all-reduce(f32[10,800]{1,0:T(8,128)S(1)} %fusion.16), channel_id=1, replica_groups=mesh['rows'=8,'pre'=4] {'pre'}, use_global_device_ids=true, to_apply=%region_4.5 | all-reduce | flops 8000 | bytes 64000 | tf_op jit(solution)/shard_map/psum | solution.py:602
  624.4 2.3 convolution_bitcast_fusion
  626.7 1.0 fusion.17
  (102 shorter events, 9.0 us)
Async XLA Ops:
  7.2 16.8 %copy-start = (bf16[1024,800]{0,1:T(8,128)(2,1)S(1)}, bf16[1024,800]{0,1:T(8,128)(2,1)}, u32[]{:S(2)}) copy-start(bf16[1024,800]{0,1:T(8,128)(2,1)} %param.38) | copy-start | bytes 4915204
  7.2 9.4 %copy-start.3 = (bf16[128,1024]{1,0:T(8,128)(2,1)S(1)}, bf16[128,1024]{1,0:T(8,128)(2,1)}, u32[]{:S(2)}) copy-start(bf16[128,1024]{1,0:T(8,128)(2,1)} %param.35) | copy-start | bytes 786436
  7.2 65.5 %all-gather.11.cloned.1.call-start = ((), (), s32[]{:S(2)}) async-start(), calls=%async_computation.2 | async-start | bytes 3244032 | tf_op jit(solution)/shard_map/all_gather | solution.py:503
  8.9 10.5 %copy-start.5 = (s32[1,1024]{1,0:T(1,128)S(1)}, s32[1,1024]{1,0:T(1,128)}, u32[]{:S(2)}) copy-start(s32[1,1024]{1,0:T(1,128)} %param.22) | copy-start | bytes 12292
  8.9 10.6 %copy-start.7 = (s32[1,1024]{1,0:T(1,128)S(1)}, s32[1,1024]{1,0:T(1,128)}, u32[]{:S(2)}) copy-start(s32[1,1024]{1,0:T(1,128)} %param.23) | copy-start | bytes 12292
  8.9 125.1 %all-gather.9.cloned.1.call-start = ((), (), s32[]{:S(2)}) async-start(), calls=%async_computation.1 | async-start | bytes 3244032 | tf_op jit(solution)/shard_map/all_gather | solution.py:503
  9.7 182.5 %all-gather.13.cloned.1.call-start = ((), (), s32[]{:S(2)}) async-start(), calls=%async_computation.3 | async-start | bytes 2162688 | tf_op jit(solution)/shard_map/all_gather | solution.py:503
  10.4 260.9 %all-gather.15.cloned.1.call-start = ((), (), s32[]{:S(2)}) async-start(), calls=%async_computation.4 | async-start | bytes 8650752 | tf_op jit(solution)/shard_map/all_gather | solution.py:503
  14.6 8.1 %copy-start.9 = (bf16[3072]{0:T(1024)(128)(2,1)S(1)}, bf16[3072]{0:T(1024)(128)(2,1)}, u32[]{:S(2)}) copy-start(bf16[3072]{0:T(1024)(128)(2,1)} %param.28) | copy-start | bytes 18436
  16.5 312.6 %all-gather.17.cloned.1.call-start = ((), (), s32[]{:S(2)}) async-start(), calls=%async_computation.5 | async-start | bytes 2162688 | tf_op jit(solution)/shard_map/all_gather | solution.py:503
  17.3 369.8 %all-gather.19.cloned.1.call-start = ((), (), s32[]{:S(2)}) async-start(), calls=%async_computation.6 | async-start | bytes 2162688 | tf_op jit(solution)/shard_map/all_gather | solution.py:503
  17.9 427.4 %all-gather.21.cloned.1.call-start = ((), (), s32[]{:S(2)}) async-start(), calls=%async_computation.7 | async-start | bytes 2162688 | tf_op jit(solution)/shard_map/all_gather | solution.py:503
  18.6 485.4 %all-gather.23.cloned.1.call-start = ((), (), s32[]{:S(2)}) async-start(), calls=%async_computation.8 | async-start | bytes 2162688 | tf_op jit(solution)/shard_map/all_gather | solution.py:503
  19.4 554.5 %reduce-scatter.2.cloned.1.call-start = ((), (), s32[]{:S(2)}) async-start(), calls=%async_computation.9 | async-start | bytes 81920 | tf_op jit(solution)/shard_map/reduce_scatter | solution.py:599
  19.4 3.3 copy-start.1
  21.1 2.7 copy-start.10
  21.1 2.7 copy-start.11
  21.1 2.7 copy-start.12
  21.2 2.7 copy-start.17
  21.2 2.8 copy-start.4
  22.6 1.8 copy-start.2
  22.7 9.1 %copy-start.13 = (bf16[1024]{0:T(1024)(128)(2,1)S(1)}, bf16[1024]{0:T(1024)(128)(2,1)}, u32[]{:S(2)}) copy-start(bf16[1024]{0:T(1024)(128)(2,1)} %param.31) | copy-start | bytes 6148
  22.7 9.7 %copy-start.14 = (bf16[1024]{0:T(1024)(128)(2,1)S(1)}, bf16[1024]{0:T(1024)(128)(2,1)}, u32[]{:S(2)}) copy-start(bf16[1024]{0:T(1024)(128)(2,1)} %param.32) | copy-start | bytes 6148
  22.7 10.2 %copy-start.15 = (bf16[1024]{0:T(1024)(128)(2,1)S(1)}, bf16[1024]{0:T(1024)(128)(2,1)}, u32[]{:S(2)}) copy-start(bf16[1024]{0:T(1024)(128)(2,1)} %param.30) | copy-start | bytes 6148
  22.7 10.8 %copy-start.8 = (bf16[4096]{0:T(1024)(128)(2,1)S(1)}, bf16[4096]{0:T(1024)(128)(2,1)}, u32[]{:S(2)}) copy-start(bf16[4096]{0:T(1024)(128)(2,1)} %param.34) | copy-start | bytes 24580
  23.1 11.3 %copy-start.16 = (bf16[1024]{0:T(1024)(128)(2,1)S(1)}, bf16[1024]{0:T(1024)(128)(2,1)}, u32[]{:S(2)}) copy-start(bf16[1024]{0:T(1024)(128)(2,1)} %param.36) | copy-start | bytes 6148
  23.9 15.4 %copy-start.6 = (f32[1024]{0:T(1024)}, f32[1024]{0:T(1024)S(1)}, u32[]{:S(2)}) copy-start(f32[1024]{0:T(1024)S(1)} %convert_element_type.82) | copy-start | bytes 12292
Sparse Core Ops, SparseCore 0:
  10.9 61.7 all-gather.10
  76.2 57.8 all-gather.8
  136.9 55.2 all-gather.12
  194.9 76.4 all-gather.14
  274.1 54.9 all-gather.16
  331.8 55.2 all-gather.18
  390.0 55.2 all-gather.20
  448.7 55.2 all-gather.22
  555.5 18.3 reduce-scatter.1
